TPU v7x, 128 devices: a whole 4x4x4 slice. The times are simulated.
128 devices in a mesh: seq: 64 (over y, z, x_hi, core), head: 2 (over x_lo).
Axes of the slice: x: 4 (x_hi: 2, x_lo: 2; x = x_hi * 2 + x_lo), y: 4, z: 4, core: 2. Of those that a mesh axis runs over, the one named last changes fastest.
Arguments:
- activations: bfloat16 [512, 256, 768], P('seq'), may hold values from -13 to 13
- w_query: bfloat16 [768, 768], P(None, 'head'), may hold values from -0.21875 to 0.21875
- w_key: bfloat16 [768, 768], P(None, 'head'), may hold values from -0.21875 to 0.21875
- w_value: bfloat16 [768, 768], P(None, 'head'), may hold values from -0.21875 to 0.21875
- w_out: bfloat16 [768, 768], P('head'), may hold values from -0.21875 to 0.21875
- cotangent: bfloat16 [512, 256, 768], P('seq'), may hold values from -6 to 6
Outputs:
- output: bfloat16 [512, 256, 768], P('seq', None, 'head')
- input_grad: bfloat16 [512, 256, 768], P('seq', None, 'head')
All inputs are finite; a program needn't handle non-finite values.
Results may differ from a plain program's by a relative error of at most 0.013.
Values may be sent and summed in bfloat16 or wider, within the bound.
A program may use at most 128 MiB of HBM per device.

v0:
```python
import math

import jax
import jax.numpy as jnp
from jax import lax
from jax.sharding import PartitionSpec as P

HEAD_DIM = 64


def softmax_rows(logits):
    top = jnp.max(logits, axis=-1, keepdims=True)
    expd = jnp.exp(logits - top)
    return (expd / jnp.sum(expd, axis=-1, keepdims=True)).astype(jnp.bfloat16)


def logit_grad(probs, dprob, scale):
    pfloat = probs.astype(jnp.float32)
    inner = jnp.sum(pfloat * dprob, axis=-1, keepdims=True)
    return (pfloat * (dprob - inner) * scale).astype(jnp.bfloat16)


def pair_sums(left, right):
    return jnp.einsum("sihc,sjhc->ihj", left, right, preferred_element_type=jnp.float32)


def on_device(activations, w_query, w_key, w_value, w_out, cotangent):
    seq_dev, residues, width = activations.shape
    local_width = w_query.shape[1]
    heads_local = local_width // HEAD_DIM
    total_seqs = seq_dev * lax.axis_size("seq")
    scale = 1.0 / (math.sqrt(HEAD_DIM) * math.sqrt(total_seqs))
    flat = activations.reshape(-1, width)

    def project(weight):
        moved = jnp.dot(flat, weight, preferred_element_type=jnp.float32).astype(jnp.bfloat16)
        return moved.reshape(seq_dev, residues, heads_local, HEAD_DIM)

    query = project(w_query)
    keys_all = project(w_key)
    values = project(w_value)
    logits = lax.psum(pair_sums(query, keys_all) * scale, "seq")
    probs = softmax_rows(logits)
    attended = jnp.einsum(
        "ihj,sjhc->sihc", probs, values, preferred_element_type=jnp.float32
    ).astype(jnp.bfloat16)
    partial_out = jnp.dot(
        attended.reshape(-1, local_width), w_out, preferred_element_type=jnp.float32
    )
    partial_out = partial_out.reshape(seq_dev, residues, width)
    output = lax.psum_scatter(partial_out, "head", scatter_dimension=2, tiled=True).astype(
        jnp.bfloat16
    )
    grad_attended = jnp.dot(
        cotangent.reshape(-1, width), w_out.T, preferred_element_type=jnp.float32
    )
    grad_attended = grad_attended.astype(jnp.bfloat16).reshape(
        seq_dev, residues, heads_local, HEAD_DIM
    )
    dprob = lax.psum(pair_sums(grad_attended, values), "seq")
    grad_logits = logit_grad(probs, dprob, scale)
    grad_query = jnp.einsum(
        "ihj,sjhc->sihc", grad_logits, keys_all, preferred_element_type=jnp.float32
    ).astype(jnp.bfloat16)
    grad_key = jnp.einsum(
        "ihj,sihc->sjhc", grad_logits, query, preferred_element_type=jnp.float32
    ).astype(jnp.bfloat16)
    grad_value = jnp.einsum(
        "ihj,sihc->sjhc", probs, grad_attended, preferred_element_type=jnp.float32
    ).astype(jnp.bfloat16)

    def back(grad, weight):
        return jnp.dot(grad.reshape(-1, local_width), weight.T, preferred_element_type=jnp.float32)

    partial_in = back(grad_query, w_query) + back(grad_key, w_key) + back(grad_value, w_value)
    partial_in = partial_in.reshape(seq_dev, residues, width)
    input_grad = lax.psum_scatter(partial_in, "head", scatter_dimension=2, tiled=True).astype(
        jnp.bfloat16
    )
    return (output, input_grad)


def solution(mesh):
    placed = (
        P("seq", None, None),
        P(None, "head"),
        P(None, "head"),
        P(None, "head"),
        P("head", None),
        P("seq", None, None),
    )
    return jax.shard_map(
        on_device,
        mesh=mesh,
        in_specs=placed,
        out_specs=(P("seq", None, "head"), P("seq", None, "head")),
        check_vma=False,
    )
```

profile of v0, /device:TPU:1, one launch (start us, length us, event | category | flops | bytes accessed | tf_op | source)
XLA Modules:
  0.0 876.2 jit_solution(15263341759510609248)
XLA Ops:
  7.2 1.8 copy-done
  9.1 4.0 convolution_convert_fusion.1
  13.1 2.6 copy.22
  15.6 3.1 copy.62
  18.8 2.9 convolution_convert_fusion.2
  21.7 2.6 copy.21
  24.3 3.1 copy.61
  27.4 2.9 convolution_convert_fusion.3
  30.3 1.7 copy.20
  32.1 1.6 copy.60
  33.7 3.7 convolution_convert_fusion
  39.6 1.0 copy-done.5
  40.7 1.8 fusion.5
  42.5 1.8 convolution_bitcast_fusion
  44.6 648.3 %all-reduce.3.cloned.1.call-done = (f32[256,6,256]{0,2,1:T(8,128)}, f32[256,6,256]{0,2,1:T(8,128)}) async-done(((f32[256,6,256]{0,2,1:T(8,128)}, f32[256,6,256]{0,2,1:T(8,128)}), (f32[256,6,256]{0,2,1:T(8,128)}, f32[256,6,256]{0,2,1:T(8,128)})) %all-reduce.3.cloned.1.call-update) | async-done | bytes 3145744 | tf_op jit(solution)/shard_map/psum | solution.py:42
  692.9 2.2 fusion.35
  695.3 1.2 copy-done.8
  697.5 1.0 copy-done.12
  698.5 4.5 fusion.29
  703.1 1.3 copy-done.6
  704.4 4.5 fusion.13
  708.9 2.3 copy.34
  711.7 4.8 fusion.16
  716.5 0.9 copy.37
  719.6 0.9 copy.40
  721.6 1.8 fusion.37
  723.5 1.8 fusion.36
  725.4 4.7 add_add_fusion
  730.1 53.4 %reduce-scatter.3.cloned.1.call-done = f32[8,256,384]{2,1,0:T(8,128)} async-done(((f32[8,256,768]{2,1,0:T(8,128)}), f32[8,256,384]{2,1,0:T(8,128)}) %reduce-scatter.3.cloned.1.call-update) | async-done | bytes 3145744 | tf_op jit(solution)/shard_map/reduce_scatter | solution.py:51
  783.5 3.4 convert_element_type.57
  786.8 79.6 %reduce-scatter.5.cloned.1.call-done = f32[8,256,384]{2,1,0:T(8,128)} async-done(((f32[8,256,768]{2,1,0:T(8,128)}), f32[8,256,384]{2,1,0:T(8,128)}) %reduce-scatter.5.cloned.1.call-update) | async-done | bytes 3145744 | tf_op jit(solution)/shard_map/reduce_scatter | solution.py:77
  866.4 3.2 convert_element_type.67
  (46 shorter events, 7.4 us)
Async XLA Ops:
  7.2 1.9 copy-start
  7.2 685.8 %all-reduce.3.cloned.1.call-start = ((), (), s32[]{:S(2)}) async-start(), calls=%async_computation.4 | async-start | bytes 6291456 | tf_op jit(solution)/shard_map/psum | solution.py:42
  15.6 3.1 copy-start.13
  24.3 3.1 copy-start.16
  32.1 1.7 copy-start.11
  38.2 1.4 copy-start.2
  38.2 2.4 copy-start.5
  38.7 3.8 copy-start.3
  40.7 1.8 copy-start.7
  44.4 739.1 %reduce-scatter.3.cloned.1.call-start = ((), (), s32[]{:S(2)}) async-start(), calls=%async_computation.2 | async-start | bytes 9437184 | tf_op jit(solution)/shard_map/reduce_scatter | solution.py:51
  695.2 1.4 copy-start.8
  696.6 0.9 copy-start.9
  697.4 1.1 copy-start.12
  703.0 1.4 copy-start.6
  703.0 163.4 %reduce-scatter.5.cloned.1.call-start = ((), (), s32[]{:S(2)}) async-start(), calls=%async_computation.3 | async-start | bytes 9437184 | tf_op jit(solution)/shard_map/reduce_scatter | solution.py:77
  717.4 1.4 copy-start.4
  717.4 1.6 copy-start.10
  720.6 1.1 copy-start.14
  721.6 1.8 copy-start.15
  723.5 1.9 copy-start.17
  783.5 86.2 %copy-start.1 = (bf16[8,256,768]{2,1,0:T(8,128)(2,1)S(1)}, bf16[8,256,768]{2,1,0:T(8,128)(2,1)}, u32[]{:S(2)}) copy-start(bf16[8,256,768]{2,1,0:T(8,128)(2,1)} %param.6) | copy-start | bytes 9437188
Sparse Core Ops, SparseCore 0:
  44.5 648.4 all-reduce.2
  703.1 80.2 reduce-scatter.2
  785.9 80.5 reduce-scatter.4
where the time goes:
time: 877 us; the launch traced here: 876 us
  waiting for transfers between devices  781 us (89%)
  matrix products  40.6 us (5%)
  local copies, waits for them, and re-layouts  31 us (4%)
  between operations  14 us (2%)
  other arithmetic  8.97 us (1%)
    psum x1, waiting for transfers between devices, on_device(): logits = lax.psum(pair_sums(query, keys_all) * scale, 'seq')  648 us
    reduce_scatter x1, waiting for transfers between devices, on_device(): lax.psum_scatter(partial_in, 'head', scatter_dimension=2, tiled=True)  79.6 us
    reduce_scatter x1, waiting for transfers between devices, on_device(): lax.psum_scatter(partial_out, 'head', scatter_dimension=2, tiled=True)  53.4 us
    unnamed x43, local copies, waits for them, and re-layouts  19.1 us
  transfers between devices with their start and end apart: 3, of which 3 were waited for; matrix products, arithmetic and copies ran while one was open for 3% of the time, Pallas kernels for 0%

commit v1 on v0

v1 whole, which is shorter than its diff:
```python
import functools
import math

import jax
import jax.numpy as jnp
from jax import lax
from jax.experimental import pallas as pl
from jax.experimental.pallas import tpu as pltpu
from jax.sharding import PartitionSpec as P

MESH = pl.DeviceIdType.MESH
BF, F32 = jnp.bfloat16, jnp.float32
S, R, D, HW, HD = 8, 256, 768, 384, 64
NT = (((1,), (1,)), ((), ()))
NN = (((1,), (0,)), ((), ()))
OWN = (0, 384, 768)
OTH = (1920, 1536, 1152)


def dot(a, b, dims=NN):
    return lax.dot_general(a, b, dims, preferred_element_type=F32)


def low_half(shape):
    return lax.broadcasted_iota(jnp.int32, shape, 1) < HD


def kernel(scale, act_hbm, wq_hbm, wk_hbm, wv_hbm, wo_hbm, cot_hbm, out_hbm, ig_hbm,
           act, cot, wn, ws, won, wos, xf, g2a, g2b, igp, keep, xs, xr, rsend, rrecv, pbuf, gat, outv, igv,
           load_sem, w_ss, w_rs, wc_ss, wc_rs, xc_ss, xc_rs, rs_ss, rs_rs, p_ss, p_rs,
           a1_ss, a1_rs, a2_ss, a2_rs, gc_ss, gc_rs, o_sem):
    seq, h = lax.axis_index("seq"), lax.axis_index("head")
    c, xh, z, y = seq % 2, (seq // 2) % 2, (seq // 4) % 4, seq // 16
    x = xh * 2 + h

    def dev(yy, zz, xx, cc):
        return (((yy % 4) * 4 + zz % 4) * 2 + (xx % 4) // 2) * 2 + cc, xx % 2

    sibling = dev(y, z, x, 1 - c)

    def remote(src, dst, ss, rs, to):
        return pltpu.make_async_remote_copy(
            src_ref=src, dst_ref=dst, send_sem=ss, recv_sem=rs, device_id=to, device_id_type=MESH)

    loads = [
        pltpu.make_async_copy(wq_hbm, wn.at[:, 0:384], load_sem.at[16]),
        pltpu.make_async_copy(wk_hbm, wn.at[:, 384:768], load_sem.at[17]),
        pltpu.make_async_copy(wv_hbm, wn.at[:, 768:1152], load_sem.at[18]),
        pltpu.make_async_copy(wo_hbm, won.at[0:384], load_sem.at[19]),
    ]

    def load_seq(hbm, buf, s, sem):
        return pltpu.make_async_copy(hbm.at[s], buf.at[s], load_sem.at[sem])

    loads[0].start()
    loads[1].start()
    for t in range(4):
        load_seq(act_hbm, act, t, t).start()
        load_seq(act_hbm, act, t + 4, t + 4).start()
    loads[2].start()
    loads[3].start()
    for s in range(S):
        load_seq(cot_hbm, cot, s, 8 + s).start()

    bar = pltpu.get_barrier_semaphore()

    def greet(to):
        pl.semaphore_signal(bar, inc=1, device_id=to, device_id_type=MESH)

    greet(sibling)

    def greet_rs(d, _):
        greet(dev(y + d // 8, z + (d // 2) % 4, x + 2 * (d % 2), c))
        return 0

    lax.fori_loop(1, 32, greet_rs, 0)

    def greet_odd(d, _):
        greet(dev(y, z + d // 2, x + 1 + 2 * (d % 2), c))
        return 0

    lax.fori_loop(0, 8, greet_odd, 0)

    def greet_odd_y(d, _):
        greet(dev(y + d // 2, z, x + 1 + 2 * (d % 2), c))
        return 0

    lax.fori_loop(2, 8, greet_odd_y, 0)

    def swap_lanes(first, count):
        def rows(r, _):
            at = pl.ds(r * 128, 128)
            for j in range(first, first + count):
                block = wn[at, 128 * j:128 * j + 128]
                ws[at, 128 * j:128 * j + 128] = jnp.concatenate([block[:, HD:], block[:, :HD]], axis=1)
            return 0
        lax.fori_loop(0, 6, rows, 0)

    def swap_rows(base):
        for g in range(3):
            at = base + 128 * g
            wos[at:at + 64, :] = won[at + 64:at + 128, :]
            wos[at + 64:at + 128, :] = won[at:at + 64, :]

    def put(kind, head, t, even, odd):
        low = low_half(even.shape)
        lanes = pl.ds(pl.multiple_of(t * 128, 128), 128)
        xf[kind, head, :, lanes] = jnp.where(low, even, odd)
        xf[kind, head + 1, :, lanes] = jnp.where(low, odd, even)

    def project(t, lanes, places):
        even = dot(act[t], wn[:, lanes[0]:lanes[1]]).astype(BF)
        odd = dot(act[t + 4], ws[:, lanes[0]:lanes[1]]).astype(BF)
        for j, (kind, head) in enumerate(places):
            put(kind, head, t, even[:, 128 * j:128 * j + 128], odd[:, 128 * j:128 * j + 128])

    def project_ga(t, half):
        even = dot(cot[t], won[384 * half:384 * half + 384, :], NT).astype(BF)
        odd = dot(cot[t + 4], wos[384 * half:384 * half + 384, :], NT).astype(BF)
        for g in range(3):
            put(3, 6 * half + 2 * g, t, even[:, 128 * g:128 * g + 128], odd[:, 128 * g:128 * g + 128])

    loads[0].wait()
    loads[1].wait()
    swap_lanes(0, 6)

    def own_qk(t, _):
        load_seq(act_hbm, act, t, t).wait()
        load_seq(act_hbm, act, t + 4, t + 4).wait()
        project(t, (0, 768), [(0, 0), (0, 2), (0, 4), (1, 0), (1, 2), (1, 4)])
        return 0

    lax.fori_loop(0, 4, own_qk, 0)

    pl.semaphore_wait(bar, 46)

    def weight_copies():
        out = []
        for way, to in ((0, dev(y, z, x + 1, c)), (1, dev(y, z, x + 3, c))):
            rows = pl.ds(pl.multiple_of((2 * c + way) * 192, 192), 192)
            for i, src in enumerate((wq_hbm, wk_hbm, wv_hbm)):
                out.append(remote(src.at[rows], wn.at[rows, OTH[i]:OTH[i] + 384], w_ss.at[way, i], w_rs.at[way, i], to))
            rows = pl.ds(pl.multiple_of((2 * c + way) * 96, 96), 96)
            dst = pl.ds(pl.multiple_of(384 + (2 * c + way) * 96, 96), 96)
            out.append(remote(wo_hbm.at[rows], won.at[dst], w_ss.at[way, 3], w_rs.at[way, 3], to))
        return out

    def weight_forwards():
        out = []
        rows = pl.ds(pl.multiple_of(c * 384, 384), 384)
        for i in range(3):
            ref = wn.at[rows, OTH[i]:OTH[i] + 384]
            out.append(remote(ref, ref, wc_ss.at[i], wc_rs.at[i], sibling))
        ref = won.at[pl.ds(pl.multiple_of(384 + c * 192, 192), 192)]
        out.append(remote(ref, ref, wc_ss.at[3], wc_rs.at[3], sibling))
        return out

    for copy in weight_copies():
        copy.start()

    def pair_sum(left, right, owner):
        def head(i, _):
            total = dot(xf[left, i], xf[right, i], NT)

            @pl.when(c == owner)
            def _():
                keep[pl.ds(pl.multiple_of(i * 256, 256), 256), :] = total

            @pl.when(c != owner)
            def _():
                xs[pl.ds(pl.multiple_of(i * 256, 256), 256), :] = total.astype(BF)
            return 0
        lax.fori_loop(0, 6, head, 0)

    core_copy = remote(xs, xr, xc_ss, xc_rs, sibling)

    pair_sum(0, 1, 0)

    @pl.when(c == 1)
    def _():
        core_copy.start()

    loads[2].wait()
    swap_lanes(6, 3)
    loads[3].wait()
    swap_rows(0)

    def own_v(t, _):
        project(t, (768, 1152), [(2, 0), (2, 2), (2, 4)])
        return 0

    lax.fori_loop(0, 4, own_v, 0)

    me = (y * 4 + z) * 2 + xh

    def rs_copy(d):
        yy, zz, hh = (y + d // 8) % 4, (z + (d // 2) % 4) % 4, (xh + d % 2) % 2
        n = (yy * 4 + zz) * 2 + hh
        return remote(rsend.at[:, n], rrecv.at[d], rs_ss.at[d], rs_rs.at[d], dev(yy, zz, hh * 2 + h, c))

    def send_sums():
        core_copy.wait_recv()

        def add(i, _):
            at = pl.ds(pl.multiple_of(i * 256, 256), 256)
            total = (keep[at, :] + xr[at, :].astype(F32)).astype(BF)
            rsend[i // 2, pl.ds((i % 2) * 16, 16)] = total.reshape(16, 16, 256)
            return 0

        lax.fori_loop(0, 6, add, 0)

        def start(d, _):
            rs_copy(d).start()
            return 0

        lax.fori_loop(1, 32, start, 0)

    def take_sums():
        def wait(d, _):
            rs_copy(d).wait_recv()
            return 0

        lax.fori_loop(1, 32, wait, 0)

        def add(d, total):
            return total + rrecv[d].astype(F32)

        return lax.fori_loop(1, 32, add, rsend[:, me].astype(F32))

    def a1_copy(k, d):
        ref = gat.at[c, h, k, y, z, xh]
        u, v = d // 4, d % 4
        to = (dev(y + u, z + v, x, c), dev(y, z + u, x + v, c), dev(y + u, z, x + v, c))[k]
        return remote(ref, ref, a1_ss.at[k, d], a1_rs.at[k, d], to)

    def gather_own(block):
        for k in range(3):
            gat[c, h, k, y, z, xh] = block[k]

        def start(d, _):
            for k in range(3):
                a1_copy(k, d).start()
            return 0

        lax.fori_loop(1, 16, start, 0)

    def plane(k, yy, zz, xx):
        if k == 0:
            return gat.at[c, xx % 2, 0, :, :, xx // 2]
        if k == 1:
            return gat.at[c, :, 1, yy]
        return gat.at[c, :, 2, :, zz]

    def a2_copy(k, d):
        ref = plane(k, y, z, x)
        to = (dev(y, z, x + d, c), dev(y + d, z, x, c), dev(y, z + d, x, c))[k]
        return remote(ref, ref, a2_ss.at[k, d], a2_rs.at[k, d], to)

    def forward(k, d):
        ref = plane(k, (y + 4 - d) % 4, (z + 4 - d) % 4, (x + 4 - d) % 4)
        return remote(ref, ref, gc_ss.at[k, d], gc_rs.at[k, d], sibling)

    def gather_planes():
        for k in range(3):
            def wait(d, _):
                a1_copy(k, d).wait_recv()
                return 0

            lax.fori_loop(1, 16, wait, 0)
            for d in (2, 1, 3):
                a2_copy(k, d).start()
            forward(k, 0).start()

    def gather_rest():
        for d in (1, 3, 2):
            for k in range(3):
                a2_copy(k, d).wait_recv()
                forward(k, d).start()

    def gather_other():
        for k in range(3):
            for d in range(4):
                forward(k, d).wait_recv()

    p_copy = remote(pbuf, pbuf, p_ss, p_rs, sibling)

    def softmax_step():
        logits = take_sums() * scale
        top = jnp.max(logits, axis=-1, keepdims=True)
        expd = jnp.exp(logits - top)
        probs = (expd / jnp.sum(expd, axis=-1, keepdims=True)).astype(BF)
        pbuf[...] = probs
        p_copy.start()
        gather_own(probs)

    def grad_step():
        dprob = take_sums()
        p_copy.wait_recv()
        probs = pbuf[...].astype(F32)
        inner = jnp.sum(probs * dprob, axis=-1, keepdims=True)
        gather_own((probs * (dprob - inner) * scale).astype(BF))

    def on_core(core, step):
        pl.when(c == core)(step)

    on_core(0, send_sums)

    def own_ga(t, _):
        load_seq(cot_hbm, cot, t, 8 + t).wait()
        load_seq(cot_hbm, cot, t + 4, 12 + t).wait()
        project_ga(t, 0)
        return 0

    lax.fori_loop(0, 4, own_ga, 0)
    pair_sum(3, 2, 1)
    on_core(0, core_copy.start)
    on_core(1, send_sums)

    for copy in weight_copies():
        copy.wait_recv()
    for copy in weight_forwards():
        copy.start()
    on_core(0, softmax_step)
    for copy in weight_forwards():
        copy.wait_recv()
    swap_lanes(9, 9)
    swap_rows(384)

    def other_qkv(t, _):
        project(t, (1152, 2304),
                [(2, 6), (2, 8), (2, 10), (1, 6), (1, 8), (1, 10), (0, 6), (0, 8), (0, 10)])
        return 0

    def other_ga(t, _):
        project_ga(t, 1)
        return 0

    lax.fori_loop(0, 2, other_qkv, 0)
    on_core(1, grad_step)
    on_core(0, gather_planes)
    lax.fori_loop(2, 4, other_qkv, 0)
    lax.fori_loop(0, 4, other_ga, 0)
    on_core(1, gather_planes)
    on_core(0, gather_rest)
    on_core(1, gather_other)

    def pair_of(arr, g):
        half = (h + g // 3) % 2
        block = gat[arr, half, g % 3].reshape(512, 256)
        return block[:256], block[256:]

    def unput(first, second, refs):
        first, second = first.astype(BF), second.astype(BF)
        low = low_half((256, 128))
        for t in range(4):
            one, two = first[:, 128 * t:128 * t + 128], second[:, 128 * t:128 * t + 128]
            ref, lanes = refs
            ref[t, :, lanes] = jnp.where(low, one, two)
            ref[t + 4, :, lanes] = jnp.where(low, two, one)

    def lanes_at(start):
        return pl.ds(pl.multiple_of(start, 128), 128)

    att, gv = act, cot

    def with_probs(g, _):
        p0, p1 = pair_of(0, g)
        at = lanes_at(128 * g)
        unput(dot(p0, xf[2, 2 * g]), dot(p1, xf[2, 2 * g + 1]), (att, at))
        unput(dot(p0.T, xf[3, 2 * g]), dot(p1.T, xf[3, 2 * g + 1]), (gv, at))
        return 0

    lax.fori_loop(0, 6, with_probs, 0)

    own_cols = pl.ds(pl.multiple_of(h * 384, 384), 384)

    def out_copy(s):
        return pltpu.make_async_copy(outv.at[s], out_hbm.at[s], o_sem.at[s])

    def ig_copy(s):
        return pltpu.make_async_copy(igv.at[s], ig_hbm.at[s], o_sem.at[8 + s])

    def from_probs(t, _):
        for s, w_o, w in ((t, won, wn), (t + 4, wos, ws)):
            outv[s] = dot(att[s], w_o[:, own_cols]).astype(BF)
            out_copy(s).start()
            igp[s] = dot(gv[s], w[own_cols, 768:1536], NT)
        return 0

    lax.fori_loop(0, 4, from_probs, 0)
    on_core(1, gather_rest)
    on_core(0, gather_other)

    def with_grads(g, _):
        l0, l1 = pair_of(1, g)
        gq0, gq1 = dot(l0, xf[1, 2 * g]), dot(l1, xf[1, 2 * g + 1])
        gk0, gk1 = dot(l0.T, xf[0, 2 * g]), dot(l1.T, xf[0, 2 * g + 1])

        @pl.when(g < 3)
        def _():
            unput(gq0, gq1, (g2a, lanes_at(128 * g)))
            unput(gk0, gk1, (g2a, lanes_at(384 + 128 * g)))

        @pl.when(g >= 3)
        def _():
            unput(gk0, gk1, (g2b, lanes_at(128 * (g - 3))))
            unput(gq0, gq1, (g2b, lanes_at(384 + 128 * (g - 3))))
        return 0

    lax.fori_loop(0, 6, with_grads, 0)

    def from_grads(t, _):
        for s, w in ((t, wn), (t + 4, ws)):
            total = igp[s] + dot(g2a[s], w[own_cols, 0:768], NT) + dot(g2b[s], w[own_cols, 1536:2304], NT)
            igv[s] = total.astype(BF)
            ig_copy(s).start()
        return 0

    lax.fori_loop(0, 4, from_grads, 0)

    for copy in weight_copies() + weight_forwards():
        copy.wait_send()
    core_copy.wait_send()
    on_core(0, p_copy.wait_send)

    def rs_left(d, _):
        rs_copy(d).wait_send()
        return 0

    lax.fori_loop(1, 32, rs_left, 0)

    def a1_left(d, _):
        for k in range(3):
            a1_copy(k, d).wait_send()
        return 0

    lax.fori_loop(1, 16, a1_left, 0)
    for k in range(3):
        for d in range(4):
            if d:
                a2_copy(k, d).wait_send()
            forward(k, d).wait_send()

    def out_left(s, _):
        out_copy(s).wait()
        ig_copy(s).wait()
        return 0

    lax.fori_loop(0, S, out_left, 0)


def on_device(total_seqs, activations, w_query, w_key, w_value, w_out, cotangent):
    scale = 1.0 / (math.sqrt(HD) * math.sqrt(total_seqs))
    hbm = pl.BlockSpec(memory_space=pl.ANY)
    dma = pltpu.SemaphoreType.DMA
    result = jax.ShapeDtypeStruct((S, R, HW), BF)
    return pl.pallas_call(
        functools.partial(kernel, scale),
        out_shape=(result, result),
        in_specs=[hbm] * 6,
        out_specs=(hbm, hbm),
        scratch_shapes=[
            pltpu.VMEM((S, R, D), BF),
            pltpu.VMEM((S, R, D), BF),
            pltpu.VMEM((D, 6 * HW), BF),
            pltpu.VMEM((D, 6 * HW), BF),
            pltpu.VMEM((D, D), BF),
            pltpu.VMEM((D, D), BF),
            pltpu.VMEM((4, 12, R, 512), BF),
            pltpu.VMEM((S, R, D), BF),
            pltpu.VMEM((S, R, D), BF),
            pltpu.VMEM((S, R, HW), F32),
            pltpu.VMEM((6 * R, R), F32),
            pltpu.VMEM((6 * R, R), BF),
            pltpu.VMEM((6 * R, R), BF),
            pltpu.VMEM((3, 32, 16, R), BF),
            pltpu.VMEM((32, 3, 16, R), BF),
            pltpu.VMEM((3, 16, R), BF),
            pltpu.VMEM((2, 2, 3, 4, 4, 2, 16, R), BF),
            pltpu.VMEM((S, R, HW), BF),
            pltpu.VMEM((S, R, HW), BF),
            dma((20,)),
            dma((2, 4)), dma((2, 4)), dma((4,)), dma((4,)),
            dma, dma,
            dma((32,)), dma((32,)),
            dma, dma,
            dma((3, 16)), dma((3, 16)), dma((3, 4)), dma((3, 4)), dma((3, 4)), dma((3, 4)),
            dma((16,)),
        ],
        compiler_params=pltpu.CompilerParams(
            collective_id=0, has_side_effects=True, vmem_limit_bytes=62 * 2**20),
        cost_estimate=pl.CostEstimate(flops=18_500_000_000, bytes_accessed=15_000_000, transcendentals=12288),
        name="tied_row_attention",
    )(activations, w_query, w_key, w_value, w_out, cotangent)


def solution(mesh):
    total_seqs = S * mesh.shape["seq"]
    placed = (
        P("seq", None, None),
        P(None, "head"),
        P(None, "head"),
        P(None, "head"),
        P("head", None),
        P("seq", None, None),
    )
    return jax.shard_map(
        functools.partial(on_device, total_seqs),
        mesh=mesh,
        in_specs=placed,
        out_specs=(P("seq", None, "head"), P("seq", None, "head")),
        check_vma=False,
    )
```

time: 877 us -> 78.3 us (0.09)
  waiting for transfers between devices: 781 us -> 0 us
  Pallas kernels: 0 us -> 72.2 us
  matrix products: 40.6 us -> 0 us
  local copies, waits for them, and re-layouts: 31 us -> 3.97 us
  between operations: 14 us -> 0.65 us
  other arithmetic: 8.97 us -> 0 us
    psum x1 -> x0, waiting for transfers between devices: 648 us -> none  [on_device(): logits = lax.psum(pair_sums(query, keys_all) * scale, 'seq')]
    reduce_scatter x2 -> x0, waiting for transfers between devices: 133 us -> none  [the longest x1 79.6 us: on_device(): lax.psum_scatter(partial_in, 'head', scatter_dimension=2, tiled=True)]
    pallas_call x0 -> x1, Pallas kernels: none -> 72.2 us  [on_device(): pl.pallas_call(functools.partial(kernel, scale), out_shape=(result, resul...]
    dot_general x14 -> x0, matrix products: 40.6 us -> none  [the longest x3 9.89 us: project(): jnp.dot(flat, weight, preferred_element_type=jnp.float32)]
    unnamed x43 -> x4, local copies, waits for them, and re-layouts: 19.1 us -> 3.97 us
    convert_element_type x8 -> x0, local copies, waits for them, and re-layouts: 11.9 us -> none  [the longest x3 6.86 us: project(): jnp.dot(flat, weight, preferred_element_type=jnp.float32)]
  transfers between devices with their start and end apart: 3 -> 0, of which waited for: 3 -> 0; matrix products, arithmetic and copies ran while one was open for 3% -> 0% of each run, Pallas kernels for 0% -> 0%
where the time goes in v1:
time: 78.3 us; the launch traced here: 76.9 us
  Pallas kernels  72.2 us (92%)
  local copies, waits for them, and re-layouts  3.97 us (5%)
    pallas_call x1, Pallas kernels, on_device(): pl.pallas_call(functools.partial(kernel, scale), out_shape=(result, resul...  72.2 us
    unnamed x4, local copies, waits for them, and re-layouts  3.97 us

profile of v1, /device:TPU:1, one launch (start us, length us, event | category | flops | bytes accessed | tf_op | source)
XLA Modules:
  0.0 76.9 jit_solution(9362993929047340188)
XLA Ops:
  0.6 72.2 %tied_row_attention.1 = (bf16[8,256,384]{2,1,0:T(8,128)(2,1)}, bf16[8,256,384]{2,1,0:T(8,128)(2,1)}) custom-call(bf16[8,256,768]{2,1,0:T(8,128)(2,1)} %act_hbm.1, bf16[768,384]{1,0:T(8,128)(2,1)} %wq_hbm.1, bf16[768,384]{1,0:T(8,128)(2,1)} %wk_hbm.1, bf16[768,384]{1,0:T(8,128)(2,1)} %wv_hbm.1, bf16[384,768]{1,0:T(8,128)(2,1)} %wo_hbm.1, ...), custom_call_target="tpu_custom_call" | custom-call | flops 18499999744 | bytes 15000000 | tf_op jit(solution)/shard_map/tied_row_attention/pallas_call | solution.py:457
  72.9 0.0 copy-start
  72.9 2.8 %copy.10 = bf16[8,256,384]{2,1,0:T(8,128)(2,1)} copy(bf16[8,256,384]{2,1,0:T(8,128)(2,1)} %get-tuple-element.4) | data formatting | bytes 3145728
  75.7 0.0 copy-done
  75.7 1.1 %copy.11 = bf16[8,256,384]{2,1,0:T(8,128)(2,1)} copy(bf16[8,256,384]{2,1,0:T(8,128)(2,1)S(1)} %copy-done) | data formatting | bytes 3145728
Async XLA Ops:
  72.9 2.8 %copy-start = (bf16[8,256,384]{2,1,0:T(8,128)(2,1)S(1)}, bf16[8,256,384]{2,1,0:T(8,128)(2,1)}, u32[]{:S(2)}) copy-start(bf16[8,256,384]{2,1,0:T(8,128)(2,1)} %get-tuple-element.5) | copy-start | bytes 4718596

commit v2 on v1

v2 whole, which is shorter than its diff:
```python
import functools
import math

import jax
import jax.numpy as jnp
from jax import lax
from jax.experimental import pallas as pl
from jax.experimental.pallas import tpu as pltpu
from jax.sharding import PartitionSpec as P

MESH = pl.DeviceIdType.MESH
BF, F32 = jnp.bfloat16, jnp.float32
S, R, D, HW, HD = 8, 256, 768, 384, 64
NT = (((1,), (1,)), ((), ()))
NN = (((1,), (0,)), ((), ()))
OWN = (0, 384, 768)
OTH = (1920, 1536, 1152)


def dot(a, b, dims=NN):
    return lax.dot_general(a, b, dims, preferred_element_type=F32)


def low_half(shape):
    return lax.broadcasted_iota(jnp.int32, shape, 1) < HD


def kernel(scale, act_hbm, wq_hbm, wk_hbm, wv_hbm, wo_hbm, cot_hbm, out_hbm, ig_hbm,
           act, cot, wn, ws, won, wos, xf, g2a, g2b, igp, keep, xs_l, xs_d, xr, rsend, rrecv, half_send, half_recv, pbuf, gat, outv, igv,
           load_sem, w_ss, w_rs, wc_ss, wc_rs, xc_ss, xc_rs, rs_ss, rs_rs, hc_ss, hc_rs, p_ss, p_rs,
           a1_ss, a1_rs, a2_ss, a2_rs, gc_ss, gc_rs, o_sem):
    seq, h = lax.axis_index("seq"), lax.axis_index("head")
    rem, div = lax.rem, lax.div
    c, xh, z, y = rem(seq, 2), rem(div(seq, 2), 2), rem(div(seq, 4), 4), div(seq, 16)
    ys, zs = [y], [z]
    for d in (1, 2, 3):
        ys.append(rem(y + d, 4))
        zs.append(rem(z + d, 4))
    x = xh * 2 + h
    xs_of = [(xh, h)]
    for d in (1, 2, 3):
        xx = rem(x + d, 4)
        xs_of.append((div(xx, 2), rem(xx, 2)))

    def dev(dy, dz, dx, cc=c):
        return ys[dy] * 16 + zs[dz] * 4 + xs_of[dx][0] * 2 + cc, xs_of[dx][1]

    sibling = dev(0, 0, 0, 1 - c)

    def remote(src, dst, ss, rs, to):
        return pltpu.make_async_remote_copy(
            src_ref=src, dst_ref=dst, send_sem=ss, recv_sem=rs, device_id=to, device_id_type=MESH)

    loads = [
        pltpu.make_async_copy(wq_hbm, wn.at[:, 0:384], load_sem.at[16]),
        pltpu.make_async_copy(wk_hbm, wn.at[:, 384:768], load_sem.at[17]),
        pltpu.make_async_copy(wv_hbm, wn.at[:, 768:1152], load_sem.at[18]),
        pltpu.make_async_copy(wo_hbm, won.at[0:384], load_sem.at[19]),
    ]

    def load_seq(hbm, buf, s, sem):
        return pltpu.make_async_copy(hbm.at[s], buf.at[s], load_sem.at[sem])

    loads[0].start()
    loads[1].start()
    for t in range(4):
        load_seq(act_hbm, act, t, t).start()
        load_seq(act_hbm, act, t + 4, t + 4).start()
    loads[2].start()
    loads[3].start()
    for s in range(S):
        load_seq(cot_hbm, cot, s, 8 + s).start()

    bar = pltpu.get_barrier_semaphore()

    def greet(to):
        pl.semaphore_signal(bar, inc=1, device_id=to, device_id_type=MESH)

    greet(sibling)
    for dy in range(4):
        for dz in range(4):
            for dx in range(4):
                if (dy, dz, dx) != (0, 0, 0) and (dx % 2 == 0 or dy == 0 or dz == 0):
                    greet(dev(dy, dz, dx))

    pl.semaphore_wait(bar, 46)

    def weight_copies():
        out = []
        for way, to in ((0, dev(0, 0, 1)), (1, dev(0, 0, 3))):
            rows = pl.ds(pl.multiple_of((2 * c + way) * 192, 192), 192)
            for i, src in enumerate((wq_hbm, wk_hbm, wv_hbm)):
                out.append(remote(src.at[rows], wn.at[rows, OTH[i]:OTH[i] + 384], w_ss.at[way, i], w_rs.at[way, i], to))
            rows = pl.ds(pl.multiple_of((2 * c + way) * 96, 96), 96)
            dst = pl.ds(pl.multiple_of(384 + (2 * c + way) * 96, 96), 96)
            out.append(remote(wo_hbm.at[rows], won.at[dst], w_ss.at[way, 3], w_rs.at[way, 3], to))
        return out

    def weight_forwards():
        out = []
        rows = pl.ds(pl.multiple_of(c * 384, 384), 384)
        for i in range(3):
            ref = wn.at[rows, OTH[i]:OTH[i] + 384]
            out.append(remote(ref, ref, wc_ss.at[i], wc_rs.at[i], sibling))
        ref = won.at[pl.ds(pl.multiple_of(384 + c * 192, 192), 192)]
        out.append(remote(ref, ref, wc_ss.at[3], wc_rs.at[3], sibling))
        return out

    for copy in weight_copies():
        copy.start()

    def swap_lanes(first, count):
        def rows(r, _):
            at = pl.ds(r * 128, 128)
            for j in range(first, first + count):
                block = wn[at, 128 * j:128 * j + 128]
                ws[at, 128 * j:128 * j + 128] = jnp.concatenate([block[:, HD:], block[:, :HD]], axis=1)
            return 0
        lax.fori_loop(0, 6, rows, 0, unroll=True)

    def swap_rows(base):
        for g in range(3):
            at = base + 128 * g
            wos[at:at + 64, :] = won[at + 64:at + 128, :]
            wos[at + 64:at + 128, :] = won[at:at + 64, :]

    def put(kind, head, t, even, odd):
        low = low_half(even.shape)
        lanes = pl.ds(pl.multiple_of(t * 128, 128), 128)
        xf[kind, head, :, lanes] = jnp.where(low, even, odd)
        xf[kind, head + 1, :, lanes] = jnp.where(low, odd, even)

    def project(t, lanes, places):
        even = dot(act[t], wn[:, lanes[0]:lanes[1]]).astype(BF)
        odd = dot(act[t + 4], ws[:, lanes[0]:lanes[1]]).astype(BF)
        for j, (kind, head) in enumerate(places):
            put(kind, head, t, even[:, 128 * j:128 * j + 128], odd[:, 128 * j:128 * j + 128])

    def project_ga(t, half):
        even = dot(cot[t], won[384 * half:384 * half + 384, :], NT).astype(BF)
        odd = dot(cot[t + 4], wos[384 * half:384 * half + 384, :], NT).astype(BF)
        for g in range(3):
            put(3, 6 * half + 2 * g, t, even[:, 128 * g:128 * g + 128], odd[:, 128 * g:128 * g + 128])

    loads[0].wait()
    loads[1].wait()
    swap_lanes(0, 6)

    def own_qk(t, _):
        load_seq(act_hbm, act, t, t).wait()
        load_seq(act_hbm, act, t + 4, t + 4).wait()
        project(t, (0, 768), [(0, 0), (0, 2), (0, 4), (1, 0), (1, 2), (1, 4)])
        return 0

    lax.fori_loop(0, 4, own_qk, 0, unroll=True)

    def pair_sum(left, right, mine, other, first):
        def head(i, _):
            total = dot(xf[left, i], xf[right, i], NT)
            at = pl.ds(pl.multiple_of(i * 256, 256), 256)
            mine[at, :] = total
            other[at, :] = total.astype(BF)
            return 0
        lax.fori_loop(first, first + 3, head, 0, unroll=True)

    def core_copy(src, part):
        at = pl.ds(part * 768, 768)
        return remote(src.at[at], xr.at[at], xc_ss.at[part], xc_rs.at[part], sibling)

    for part in (0, 1):
        pair_sum(0, 1, keep, xs_l, 3 * part)

        @pl.when(c == 1)
        def _():
            core_copy(xs_l, part).start()

    loads[2].wait()
    swap_lanes(6, 3)
    loads[3].wait()
    swap_rows(0)

    def own_v(t, _):
        project(t, (768, 1152), [(2, 0), (2, 2), (2, 4)])
        return 0

    lax.fori_loop(0, 4, own_v, 0, unroll=True)

    me = y * 4 + z

    others = [(dy, dz) for dy in range(4) for dz in range(4)][1:]

    def rs_copy(i, dy, dz):
        return remote(rsend.at[:, ys[dy] * 4 + zs[dz]], rrecv.at[i], rs_ss, rs_rs, dev(dy, dz, 0))

    rs_all = remote(rrecv, rrecv, rs_ss, rs_rs, sibling)
    half_copy = remote(half_send, half_recv, hc_ss, hc_rs, dev(0, 0, 2))

    def send_sums():
        for part in (0, 1):
            core_copy(xs_l, part).wait_recv()

            def add(i, _):
                at = pl.ds(pl.multiple_of(i * 256, 256), 256)
                total = (keep[at, :] + xr[at, :].astype(F32)).astype(BF)
                rsend[i // 2, pl.ds((i % 2) * 8, 8)] = total.reshape(8, 2, 16, 256)
                return 0

            lax.fori_loop(3 * part, 3 * part + 3, add, 0, unroll=True)
        for i, where in enumerate(others):
            rs_copy(i, *where).start()

    def take_half(half):
        def add(d, total):
            return total + rrecv[d, :, half].astype(F32)

        return lax.fori_loop(0, 15, add, rsend[:, me, half].astype(F32), unroll=True)

    def take_sums():
        rs_all.wait_recv()
        half_send[...] = take_half(1 - xh)
        half_copy.start()
        own = take_half(xh)
        half_copy.wait_recv()
        return own + half_recv[...]

    def a1_copy(k, u, v):
        ref = gat.at[c, h, k, y, z, xh]
        to = (dev(u, v, 0), dev(0, u, v), dev(u, 0, v))[k]
        return remote(ref, ref, a1_ss.at[k], a1_rs.at[k], to)

    a1_all = [remote(rrecv.at[0:5, :, 0], rrecv.at[0:5, :, 0], a1_ss.at[k], a1_rs.at[k], sibling) for k in range(3)]

    def gather_own(block):
        for k in range(3):
            gat[c, h, k, y, z, xh] = block[k]
        for u in range(4):
            for v in range(4):
                if (u, v) != (0, 0):
                    for k in range(3):
                        a1_copy(k, u, v).start()

    def plane(k, d):
        if k == 0:
            return gat.at[c, xs_of[d][1], 0, :, :, xs_of[d][0]]
        if k == 1:
            return gat.at[c, :, 1, ys[d]]
        return gat.at[c, :, 2, :, zs[d]]

    def a2_copy(k, d):
        ref = plane(k, 0)
        to = (dev(0, 0, d), dev(d, 0, 0), dev(0, d, 0))[k]
        return remote(ref, ref, a2_ss.at[k, d], a2_rs.at[k, d], to)

    def forward(k, d):
        ref = plane(k, (4 - d) % 4)
        return remote(ref, ref, gc_ss.at[k, d], gc_rs.at[k, d], sibling)

    def gather_planes():
        for k in range(3):
            a1_all[k].wait_recv()
            for d in (2, 1, 3):
                a2_copy(k, d).start()
        for k in range(3):
            forward(k, 0).start()

    def gather_rest():
        for d in (1, 3, 2):
            for k in range(3):
                a2_copy(k, d).wait_recv()
                forward(k, d).start()

    def gather_other():
        for k in range(3):
            for d in range(4):
                forward(k, d).wait_recv()

    p_copy = remote(pbuf, pbuf, p_ss, p_rs, sibling)

    def softmax_step():
        logits = take_sums() * scale
        top = jnp.max(logits, axis=-1, keepdims=True)
        expd = jnp.exp(logits - top)
        probs = (expd / jnp.sum(expd, axis=-1, keepdims=True)).astype(BF)
        pbuf[...] = probs
        p_copy.start()
        gather_own(probs)

    def grad_step():
        dprob = take_sums()
        p_copy.wait_recv()
        probs = pbuf[...].astype(F32)
        inner = jnp.sum(probs * dprob, axis=-1, keepdims=True)
        gather_own((probs * (dprob - inner) * scale).astype(BF))

    def on_core(core, step):
        pl.when(c == core)(step)

    on_core(0, send_sums)

    def own_ga(t, _):
        load_seq(cot_hbm, cot, t, 8 + t).wait()
        load_seq(cot_hbm, cot, t + 4, 12 + t).wait()
        project_ga(t, 0)
        return 0

    lax.fori_loop(0, 4, own_ga, 0, unroll=True)
    for part in (0, 1):
        pair_sum(3, 2, keep, xs_d, 3 * part)
        on_core(0, core_copy(xs_d, part).start)
    on_core(1, send_sums)

    def other_qkv(t, _):
        project(t, (1152, 2304),
                [(2, 6), (2, 8), (2, 10), (1, 6), (1, 8), (1, 10), (0, 6), (0, 8), (0, 10)])
        return 0

    def other_ga(t, _):
        project_ga(t, 1)
        return 0

    on_core(0, softmax_step)
    for copy in weight_copies():
        copy.wait_recv()
    for copy in weight_forwards():
        copy.start()
    on_core(1, grad_step)
    for copy in weight_forwards():
        copy.wait_recv()
    swap_lanes(9, 9)
    swap_rows(384)
    lax.fori_loop(0, 2, other_qkv, 0, unroll=True)
    on_core(0, gather_planes)
    lax.fori_loop(2, 4, other_qkv, 0, unroll=True)
    lax.fori_loop(0, 4, other_ga, 0, unroll=True)
    on_core(1, gather_planes)
    on_core(0, gather_rest)
    on_core(1, gather_other)

    def pair_of(arr, g):
        half = (h + g // 3) % 2
        block = gat[arr, half, g % 3].reshape(512, 256)
        return block[:256], block[256:]

    def unput(first, second, refs):
        first, second = first.astype(BF), second.astype(BF)
        low = low_half((256, 128))
        for t in range(4):
            one, two = first[:, 128 * t:128 * t + 128], second[:, 128 * t:128 * t + 128]
            ref, lanes = refs
            ref[t, :, lanes] = jnp.where(low, one, two)
            ref[t + 4, :, lanes] = jnp.where(low, two, one)

    def lanes_at(start):
        return pl.ds(pl.multiple_of(start, 128), 128)

    att, gv = act, cot

    def with_probs(g, _):
        p0, p1 = pair_of(0, g)
        at = lanes_at(128 * g)
        unput(dot(p0, xf[2, 2 * g]), dot(p1, xf[2, 2 * g + 1]), (att, at))
        unput(dot(p0.T, xf[3, 2 * g]), dot(p1.T, xf[3, 2 * g + 1]), (gv, at))
        return 0

    lax.fori_loop(0, 6, with_probs, 0, unroll=True)

    own_cols = pl.ds(pl.multiple_of(h * 384, 384), 384)

    def out_copy(s):
        return pltpu.make_async_copy(outv.at[s], out_hbm.at[s], o_sem.at[s])

    def ig_copy(s):
        return pltpu.make_async_copy(igv.at[s], ig_hbm.at[s], o_sem.at[8 + s])

    def from_probs(t, _):
        for s, w_o, w in ((t, won, wn), (t + 4, wos, ws)):
            outv[s] = dot(att[s], w_o[:, own_cols]).astype(BF)
            out_copy(s).start()
            igp[s] = dot(gv[s], w[own_cols, 768:1536], NT)
        return 0

    lax.fori_loop(0, 2, from_probs, 0, unroll=True)
    on_core(1, gather_rest)
    lax.fori_loop(2, 4, from_probs, 0, unroll=True)
    on_core(0, gather_other)

    def with_grads(ref, first, query_at, key_at):
        def pair(i, _):
            g = first + i
            l0, l1 = pair_of(1, g)
            unput(dot(l0, xf[1, 2 * g]), dot(l1, xf[1, 2 * g + 1]), (ref, lanes_at(query_at + 128 * i)))
            unput(dot(l0.T, xf[0, 2 * g]), dot(l1.T, xf[0, 2 * g + 1]), (ref, lanes_at(key_at + 128 * i)))
            return 0
        lax.fori_loop(0, 3, pair, 0, unroll=True)

    with_grads(g2a, 0, 0, 384)
    with_grads(g2b, 3, 384, 0)

    def from_grads(t, _):
        for s, w in ((t, wn), (t + 4, ws)):
            total = igp[s] + dot(g2a[s], w[own_cols, 0:768], NT) + dot(g2b[s], w[own_cols, 1536:2304], NT)
            igv[s] = total.astype(BF)
            ig_copy(s).start()
        return 0

    for copy in weight_copies() + weight_forwards():
        copy.wait_send()
    on_core(0, p_copy.wait_send)
    rs_all.wait_send()
    half_copy.wait_send()
    for k in range(3):
        a1_all[k].wait_send()
        for d in range(4):
            if d:
                a2_copy(k, d).wait_send()
            forward(k, d).wait_send()
    for part in (0, 1):
        core_copy(xs_l, part).wait_send()

    lax.fori_loop(0, 4, from_grads, 0, unroll=True)

    def out_left(s, _):
        out_copy(s).wait()
        ig_copy(s).wait()
        return 0

    lax.fori_loop(0, S, out_left, 0)


def on_device(total_seqs, activations, w_query, w_key, w_value, w_out, cotangent):
    scale = 1.0 / (math.sqrt(HD) * math.sqrt(total_seqs))
    hbm = pl.BlockSpec(memory_space=pl.ANY)
    dma = pltpu.SemaphoreType.DMA
    result = jax.ShapeDtypeStruct((S, R, HW), BF)
    return pl.pallas_call(
        functools.partial(kernel, scale),
        out_shape=(result, result),
        in_specs=[hbm] * 6,
        out_specs=(hbm, hbm),
        scratch_shapes=[
            pltpu.VMEM((S, R, D), BF),
            pltpu.VMEM((S, R, D), BF),
            pltpu.VMEM((D, 6 * HW), BF),
            pltpu.VMEM((D, 6 * HW), BF),
            pltpu.VMEM((D, D), BF),
            pltpu.VMEM((D, D), BF),
            pltpu.VMEM((4, 12, R, 512), BF),
            pltpu.VMEM((S, R, D), BF),
            pltpu.VMEM((S, R, D), BF),
            pltpu.VMEM((S, R, HW), F32),
            pltpu.VMEM((6 * R, R), F32),
            pltpu.VMEM((6 * R, R), BF),
            pltpu.VMEM((6 * R, R), BF),
            pltpu.VMEM((6 * R, R), BF),
            pltpu.VMEM((3, 16, 2, 16, R), BF),
            pltpu.VMEM((15, 3, 2, 16, R), BF),
            pltpu.VMEM((3, 16, R), F32),
            pltpu.VMEM((3, 16, R), F32),
            pltpu.VMEM((3, 16, R), BF),
            pltpu.VMEM((2, 2, 3, 4, 4, 2, 16, R), BF),
            pltpu.VMEM((S, R, HW), BF),
            pltpu.VMEM((S, R, HW), BF),
            dma((20,)),
            dma((2, 4)), dma((2, 4)), dma((4,)), dma((4,)),
            dma((2,)), dma((2,)),
            dma, dma,
            dma, dma,
            dma, dma,
            dma((3,)), dma((3,)), dma((3, 4)), dma((3, 4)), dma((3, 4)), dma((3, 4)),
            dma((16,)),
        ],
        compiler_params=pltpu.CompilerParams(
            collective_id=0, has_side_effects=True, vmem_limit_bytes=62 * 2**20),
        cost_estimate=pl.CostEstimate(flops=18_500_000_000, bytes_accessed=15_000_000, transcendentals=12288),
        name="tied_row_attention",
    )(activations, w_query, w_key, w_value, w_out, cotangent)


def solution(mesh):
    total_seqs = S * mesh.shape["seq"]
    placed = (
        P("seq", None, None),
        P(None, "head"),
        P(None, "head"),
        P(None, "head"),
        P("head", None),
        P("seq", None, None),
    )
    return jax.shard_map(
        functools.partial(on_device, total_seqs),
        mesh=mesh,
        in_specs=placed,
        out_specs=(P("seq", None, "head"), P("seq", None, "head")),
        check_vma=False,
    )
```

time: 78.3 us -> 63.4 us (0.81); the launches traced: 76.9 us -> 63.3 us
  Pallas kernels: 72.2 us -> 58.6 us
    pallas_call x1, Pallas kernels: 72.2 us -> 58.6 us  [on_device(): pl.pallas_call(functools.partial(kernel, scale), out_shape=(result, resul...]
where the time goes in v2:
time: 63.4 us; the launch traced here: 63.3 us
  Pallas kernels  58.6 us (92%)
  local copies, waits for them, and re-layouts  3.97 us (6%)
  between operations  0.65 us (1%)
    pallas_call x1, Pallas kernels, on_device(): pl.pallas_call(functools.partial(kernel, scale), out_shape=(result, resul...  58.6 us
    unnamed x4, local copies, waits for them, and re-layouts  3.97 us

profile of v2, /device:TPU:1, one launch (start us, length us, event | category | flops | bytes accessed | tf_op | source)
XLA Modules:
  0.0 63.3 jit_solution(2593477891852970934)
XLA Ops:
  0.6 58.6 %tied_row_attention.1 = (bf16[8,256,384]{2,1,0:T(8,128)(2,1)}, bf16[8,256,384]{2,1,0:T(8,128)(2,1)}) custom-call(bf16[8,256,768]{2,1,0:T(8,128)(2,1)} %act_hbm.1, bf16[768,384]{1,0:T(8,128)(2,1)} %wq_hbm.1, bf16[768,384]{1,0:T(8,128)(2,1)} %wk_hbm.1, bf16[768,384]{1,0:T(8,128)(2,1)} %wv_hbm.1, bf16[384,768]{1,0:T(8,128)(2,1)} %wo_hbm.1, ...), custom_call_target="tpu_custom_call" | custom-call | flops 18499999744 | bytes 15000000 | tf_op jit(solution)/shard_map/tied_row_attention/pallas_call | solution.py:435
  59.3 0.0 copy-start
  59.3 2.8 %copy.10 = bf16[8,256,384]{2,1,0:T(8,128)(2,1)} copy(bf16[8,256,384]{2,1,0:T(8,128)(2,1)} %get-tuple-element.4) | data formatting | bytes 3145728
  62.1 0.0 copy-done
  62.1 1.1 %copy.11 = bf16[8,256,384]{2,1,0:T(8,128)(2,1)} copy(bf16[8,256,384]{2,1,0:T(8,128)(2,1)S(1)} %copy-done) | data formatting | bytes 3145728
Async XLA Ops:
  59.3 2.8 %copy-start = (bf16[8,256,384]{2,1,0:T(8,128)(2,1)S(1)}, bf16[8,256,384]{2,1,0:T(8,128)(2,1)}, u32[]{:S(2)}) copy-start(bf16[8,256,384]{2,1,0:T(8,128)(2,1)} %get-tuple-element.5) | copy-start | bytes 4718596

commit v3 on v2

--- a/solution.py
+++ b/solution.py
@@ -183,7 +183,6 @@
         project(t, (768, 1152), [(2, 0), (2, 2), (2, 4)])
         return 0
 
-    lax.fori_loop(0, 4, own_v, 0, unroll=True)
 
     me = y * 4 + z
 
@@ -239,40 +238,43 @@
                     for k in range(3):
                         a1_copy(k, u, v).start()
 
-    def plane(k, d):
+    def plane(k, d, part):
         if k == 0:
-            return gat.at[c, xs_of[d][1], 0, :, :, xs_of[d][0]]
+            return gat.at[c, xs_of[d][1], 0, 2 * part:2 * part + 2, :, xs_of[d][0]]
         if k == 1:
-            return gat.at[c, :, 1, ys[d]]
-        return gat.at[c, :, 2, :, zs[d]]
-
-    def a2_copy(k, d):
-        ref = plane(k, 0)
+            return gat.at[c, part, 1, ys[d]]
+        return gat.at[c, part, 2, :, zs[d]]
+
+    def a2_copy(k, d, part):
+        ref = plane(k, 0, part)
         to = (dev(0, 0, d), dev(d, 0, 0), dev(0, d, 0))[k]
-        return remote(ref, ref, a2_ss.at[k, d], a2_rs.at[k, d], to)
-
-    def forward(k, d):
-        ref = plane(k, (4 - d) % 4)
-        return remote(ref, ref, gc_ss.at[k, d], gc_rs.at[k, d], sibling)
+        return remote(ref, ref, a2_ss.at[k, d, part], a2_rs.at[k, d, part], to)
+
+    def forward(k, d, part):
+        ref = plane(k, (4 - d) % 4, part)
+        return remote(ref, ref, gc_ss.at[k, d, part], gc_rs.at[k, d, part], sibling)
 
     def gather_planes():
         for k in range(3):
             a1_all[k].wait_recv()
-            for d in (2, 1, 3):
-                a2_copy(k, d).start()
+            for part in (0, 1):
+                for d in (2, 1, 3):
+                    a2_copy(k, d, part).start()
         for k in range(3):
-            forward(k, 0).start()
-
-    def gather_rest():
+            for part in (0, 1):
+                forward(k, 0, part).start()
+
+    def gather_rest(part):
         for d in (1, 3, 2):
-            for k in range(3):
-                a2_copy(k, d).wait_recv()
-                forward(k, d).start()
+            for k in (1, 2, 0):
+                a2_copy(k, d, part).wait_recv()
+                forward(k, d, part).start()
 
     def gather_other():
         for k in range(3):
             for d in range(4):
-                forward(k, d).wait_recv()
+                for part in (0, 1):
+                    forward(k, d, part).wait_recv()
 
     p_copy = remote(pbuf, pbuf, p_ss, p_rs, sibling)
 
@@ -295,7 +297,10 @@
     def on_core(core, step):
         pl.when(c == core)(step)
 
+
+    lax.fori_loop(0, 2, own_v, 0, unroll=True)
     on_core(0, send_sums)
+    lax.fori_loop(2, 4, own_v, 0, unroll=True)
 
     def own_ga(t, _):
         load_seq(cot_hbm, cot, t, 8 + t).wait()
@@ -333,7 +338,8 @@
     lax.fori_loop(2, 4, other_qkv, 0, unroll=True)
     lax.fori_loop(0, 4, other_ga, 0, unroll=True)
     on_core(1, gather_planes)
-    on_core(0, gather_rest)
+    on_core(0, functools.partial(gather_rest, 0))
+    on_core(0, functools.partial(gather_rest, 1))
     on_core(1, gather_other)
 
     def pair_of(arr, g):
@@ -379,8 +385,9 @@
             igp[s] = dot(gv[s], w[own_cols, 768:1536], NT)
         return 0
 
+    on_core(1, functools.partial(gather_rest, 0))
     lax.fori_loop(0, 2, from_probs, 0, unroll=True)
-    on_core(1, gather_rest)
+    on_core(1, functools.partial(gather_rest, 1))
     lax.fori_loop(2, 4, from_probs, 0, unroll=True)
     on_core(0, gather_other)
 
@@ -411,9 +418,10 @@
     for k in range(3):
         a1_all[k].wait_send()
         for d in range(4):
-            if d:
-                a2_copy(k, d).wait_send()
-            forward(k, d).wait_send()
+            for part in (0, 1):
+                if d:
+                    a2_copy(k, d, part).wait_send()
+                forward(k, d, part).wait_send()
     for part in (0, 1):
         core_copy(xs_l, part).wait_send()
 
@@ -466,7 +474,7 @@
             dma, dma,
             dma, dma,
             dma, dma,
-            dma((3,)), dma((3,)), dma((3, 4)), dma((3, 4)), dma((3, 4)), dma((3, 4)),
+            dma((3,)), dma((3,)), dma((3, 4, 2)), dma((3, 4, 2)), dma((3, 4, 2)), dma((3, 4, 2)),
             dma((16,)),
         ],
         compiler_params=pltpu.CompilerParams(

time: 63.4 us -> 61.4 us (0.968)
  Pallas kernels: 58.6 us -> 56.7 us
    pallas_call x1, Pallas kernels: 58.6 us -> 56.7 us  [on_device(): pl.pallas_call(functools.partial(kernel, scale), out_shape=(result, resul...]
where the time goes in v3:
time: 61.4 us; the launch traced here: 61.3 us
  Pallas kernels  56.7 us (92%)
  local copies, waits for them, and re-layouts  3.97 us (6%)
  between operations  0.65 us (1%)
    pallas_call x1, Pallas kernels, on_device(): pl.pallas_call(functools.partial(kernel, scale), out_shape=(result, resul...  56.7 us
    unnamed x4, local copies, waits for them, and re-layouts  3.97 us

profile of v3, /device:TPU:1, one launch (start us, length us, event | category | flops | bytes accessed | tf_op | source)
XLA Modules:
  0.0 61.3 jit_solution(1708195392126963832)
XLA Ops:
  0.6 56.7 %tied_row_attention.1 = (bf16[8,256,384]{2,1,0:T(8,128)(2,1)}, bf16[8,256,384]{2,1,0:T(8,128)(2,1)}) custom-call(bf16[8,256,768]{2,1,0:T(8,128)(2,1)} %act_hbm.1, bf16[768,384]{1,0:T(8,128)(2,1)} %wq_hbm.1, bf16[768,384]{1,0:T(8,128)(2,1)} %wk_hbm.1, bf16[768,384]{1,0:T(8,128)(2,1)} %wv_hbm.1, bf16[384,768]{1,0:T(8,128)(2,1)} %wo_hbm.1, ...), custom_call_target="tpu_custom_call" | custom-call | flops 18499999744 | bytes 15000000 | tf_op jit(solution)/shard_map/tied_row_attention/pallas_call | solution.py:443
  57.3 0.0 copy-start
  57.4 2.8 %copy.10 = bf16[8,256,384]{2,1,0:T(8,128)(2,1)} copy(bf16[8,256,384]{2,1,0:T(8,128)(2,1)} %get-tuple-element.4) | data formatting | bytes 3145728
  60.2 0.0 copy-done
  60.2 1.1 %copy.11 = bf16[8,256,384]{2,1,0:T(8,128)(2,1)} copy(bf16[8,256,384]{2,1,0:T(8,128)(2,1)S(1)} %copy-done) | data formatting | bytes 3145728
Async XLA Ops:
  57.3 2.8 %copy-start = (bf16[8,256,384]{2,1,0:T(8,128)(2,1)S(1)}, bf16[8,256,384]{2,1,0:T(8,128)(2,1)}, u32[]{:S(2)}) copy-start(bf16[8,256,384]{2,1,0:T(8,128)(2,1)} %get-tuple-element.5) | copy-start | bytes 4718596
